TPU v7x, 32 devices: a whole 2x2x4 slice. The times are simulated.
32 devices in a mesh: pairs: 32 (over z, y, x, core).
Axes of the slice: x: 2, y: 2, z: 4, core: 2. Of those that a mesh axis runs over, the one named last changes fastest.
Arguments:
- images: bfloat16 [16384, 1152], P('pairs'), as said below
- texts: bfloat16 [16384, 1152], P('pairs'), as said below
- labels: int32 [16384], P('pairs'), may hold values from 0 to 255
- log_scale: float32 [], replicated, may hold values from 1.8 to 2.8
- bias: float32 [], replicated, may hold values from -12 to -6
Outputs:
- loss: float32 [], replicated
- scale_grad: float32 [], replicated
- bias_grad: float32 [], replicated
- image_grad: bfloat16 [16384, 1152], P('pairs')
- text_grad: bfloat16 [16384, 1152], P('pairs')
Inputs may be any that keep to these rules, and one draw needn't show every extreme that they name: `images`: rows of length between 1 and 3. `texts`: rows of length between 1 and 3.
All inputs are finite; a program needn't handle non-finite values.
Results may differ from a plain program's by a relative error of at most 0.001.
The roundings to bfloat16 on the way count: a program that leaves them out, or rounds other values in their place, can miss the bound.
Values may be sent and summed in bfloat16 or wider, within the bound.
A program may use at most 64 MiB of HBM per device.

v0:
```python
import jax
import jax.numpy as jnp
from jax import lax
from jax.sharding import PartitionSpec as P


def from_behind(shard, axis, by):
    size = lax.axis_size(axis)
    return lax.ppermute(shard, axis, [(i, (i + by) % size) for i in range(size)])


def normalize(rows):
    return rows * lax.rsqrt(jnp.sum(rows * rows, axis=-1, keepdims=True) + 1e-06)


def tile(x_block, x_tags, y_block, y_tags, scale, bias):
    cosine = lax.dot_general(
        x_block, y_block, (((1,), (1,)), ((), ())), preferred_element_type=jnp.float32
    )
    logits = scale * cosine + bias
    sign = jnp.where(x_tags[:, None] == y_tags[None, :], 1.0, -1.0).astype(jnp.float32)
    margin = sign * logits
    summed = jnp.sum(jax.nn.softplus(-margin))
    slope = -sign * jax.nn.sigmoid(-margin)
    weighted = (scale * slope).astype(jnp.bfloat16)
    return (summed, jnp.sum(slope * (logits - bias)), jnp.sum(slope), weighted)


def transposed(weighted, x_block):
    return lax.dot_general(
        weighted, x_block, (((0,), (0,)), ((), ())), preferred_element_type=jnp.float32
    )


def per_device(images, texts, labels, log_scale, bias):
    scale = jnp.exp(log_scale)
    img32 = images.astype(jnp.float32)
    txt32 = texts.astype(jnp.float32)
    xnorm = normalize(img32).astype(jnp.bfloat16)
    ynorm = normalize(txt32).astype(jnp.bfloat16)
    tags = labels.astype(jnp.bfloat16)
    halfway = lax.axis_size("pairs") // 2
    own = tile(xnorm, tags, ynorm, tags, scale, bias)
    behind_y, behind_tags = from_behind((ynorm, tags), "pairs", 1)
    far_y, far_tags = from_behind((ynorm, tags), "pairs", halfway)
    near = tile(xnorm, tags, behind_y, behind_tags, scale, bias)
    far = tile(xnorm, tags, far_y, far_tags, scale, bias)
    near_back = from_behind(transposed(near[3], xnorm).astype(jnp.bfloat16), "pairs", -1)
    far_back = from_behind(transposed(far[3], xnorm).astype(jnp.bfloat16), "pairs", halfway)
    text_dy = (
        transposed(own[3], xnorm) + near_back.astype(jnp.float32) + far_back.astype(jnp.float32)
    )
    image_dx = jnp.dot(own[3], ynorm, preferred_element_type=jnp.float32)
    image_dx = image_dx + jnp.dot(near[3], behind_y, preferred_element_type=jnp.float32)
    image_dx = image_dx + jnp.dot(far[3], far_y, preferred_element_type=jnp.float32)
    local_totals = (own[0] + near[0] + far[0], own[1] + near[1] + far[1], own[2] + near[2] + far[2])
    summed, slope_dots, slope_sums = lax.psum(
        (local_totals[0], local_totals[1], local_totals[2]), "pairs"
    )
    count = jnp.float32(lax.axis_size("pairs") * images.shape[0])
    _, image_pull = jax.vjp(normalize, img32)
    _, text_pull = jax.vjp(normalize, txt32)
    image_grad = image_pull(image_dx)[0].astype(jnp.bfloat16)
    text_grad = text_pull(text_dy)[0].astype(jnp.bfloat16)
    return (summed / count, slope_dots / count, slope_sums / count, image_grad, text_grad)


def solution(mesh):
    placed = (P("pairs", None), P("pairs", None), P("pairs"), P(), P())
    return jax.shard_map(
        per_device,
        mesh=mesh,
        in_specs=placed,
        out_specs=(P(), P(), P(), P("pairs", None), P("pairs", None)),
        check_vma=False,
    )
```

profile of v0, /device:TPU:15, one launch (start us, length us, event | category | flops | bytes accessed | tf_op | source)
XLA Modules:
  0.0 203.5 jit_solution(10158603975017425612)
XLA Ops:
  0.6 1.7 fusion.5
  2.6 1.8 collective-permute-start.1
  4.4 0.6 collective-permute-start.3
  5.1 0.6 convert_element_type.42
  5.7 1.7 collective-permute-start.2
  7.4 0.6 collective-permute-start
  9.7 0.9 fusion.10
  10.6 43.1 %collective-permute-done.1 = bf16[512,1152]{1,0:T(8,128)(2,1)} collective-permute-done((bf16[512,1152]{1,0:T(8,128)(2,1)S(1)}, bf16[512,1152]{1,0:T(8,128)(2,1)}, u32[]{:S(2)}, u32[]{:S(2)}) %collective-permute-start.1) | collective-permute-done | bytes 1179680 | tf_op jit(solution)/shard_map/ppermute | solution.py:9
  53.7 2.2 %fusion.9 = f32[512,512]{1,0:T(8,128)S(1)} fusion(bf16[512,1152]{1,0:T(8,128)(2,1)} %collective-permute-done.1, f32[]{:T(128)S(6)} %copy.11, f32[]{:T(128)S(6)} %exp.22, bf16[512,1152]{1,0:T(8,128)(2,1)S(1)} %copy-done.1, f32[512]{0:T(512)S(1)} %add_rsqrt_fusion.1), kind=kOutput, calls=%fused_computation.35 | convolution fusion | flops 606273536 | bytes 3409928 | tf_op jit(solution)/shard_map/dot_general | solution.py:17
  55.9 12.3 %collective-permute-done.2 = bf16[512]{0:T(512)(128)(2,1)} collective-permute-done((bf16[512]{0:T(512)(128)(2,1)}, bf16[512]{0:T(512)(128)(2,1)}, u32[]{:S(2)}, u32[]{:S(2)}) %collective-permute-start.2) | collective-permute-done | bytes 1056 | tf_op jit(solution)/shard_map/ppermute | solution.py:9
  68.2 6.9 %fusion.30 = (f32[]{:T(128)}, f32[]{:T(128)}, f32[]{:T(128)}, f32[]{:T(128)}, f32[]{:T(128)}, /*index=5*/f32[]{:T(128)}, f32[]{:T(128)}, f32[]{:T(128)}, f32[]{:T(128)}, f32[512,512]{1,0:T(8,128)}) fusion(bf16[512]{0:T(512)(128)(2,1)} %collective-permute-done.2, bf16[512]{0:T(512)(128)(2,1)} %convert_element_type.42, f32[]{:T(128)S(6)} %copy.11, ...), kind=kOutput, calls=%fused_computation.57 | convolution fusion | flops 622264320 | bytes 5510188 | tf_op jit(solution)/shard_map/dot_general | solution.py:17
  80.9 3.8 %fusion.18 = f32[512,1152]{1,0:T(8,128)} fusion(bf16[512,1152]{1,0:T(8,128)(2,1)S(1)} %fusion.6, f32[]{:T(128)S(6)} %exp.22, f32[512,512]{1,0:T(8,128)} %copy-done.3, bf16[512]{0:T(512)(128)(2,1)} %convert_element_type.42), kind=kOutput, calls=%fused_computation.51 | convolution fusion | flops 606339072 | bytes 4588548 | tf_op jit(solution)/shard_map/dot_general | solution.py:53
  84.6 40.4 %all-reduce = (f32[]{:T(128)}, f32[]{:T(128)}, f32[]{:T(128)}) all-reduce(f32[]{:T(128)S(6)} %add.101, f32[]{:T(128)S(6)} %add.106, f32[]{:T(128)S(6)} %add.108), channel_id=1, replica_groups=mesh['pairs'=32] {'pairs'}, use_global_device_ids=true, to_apply=%region_5.6 | all-reduce | flops 3 | bytes 24 | tf_op jit(solution)/shard_map/psum | solution.py:57
  126.9 2.5 %convolution_convert_fusion = bf16[512,1152]{1,0:T(8,128)(2,1)S(1)} fusion(f32[]{:T(128)S(6)} %exp.22, bf16[512,1152]{1,0:T(8,128)(2,1)S(1)} %copy-done.1, f32[512]{0:T(512)S(1)} %add_rsqrt_fusion.1, f32[512,512]{1,0:T(8,128)} %get-tuple-element.23, bf16[512]{0:T(512)(128)(2,1)} %collective-permute-done.2, bf16[512]{0:T(512)(128)(2,1)} %convert_element_type.42), kind=kOutput, calls=%fused_computation.15 | convolution fusion | flops 608698368 | bytes 3411972 | tf_op jit(solution)/shard_map/dot_general | solution.py:30
  129.4 1.9 collective-permute-start.5
  131.3 1.8 convolution_convert_fusion.1
  133.1 1.5 collective-permute-start.4
  134.6 2.3 %convolution_add_fusion.1 = f32[512,1152]{1,0:T(8,128)S(1)} fusion(f32[512,1152]{1,0:T(8,128)S(1)} %copy-done.7, bf16[512,1152]{1,0:T(8,128)(2,1)} %collective-permute-done.1, f32[]{:T(128)S(6)} %exp.22, f32[512,512]{1,0:T(8,128)S(1)} %copy-done.6, bf16[512]{0:T(512)(128)(2,1)} %collective-permute-done, bf16[512]{0:T(512)(128)(2,1)} %convert_element_type.42), kind=kOutput, calls=%fused_computation.11 | convolution fusion | flops 606928896 | bytes 6948868 | tf_op jit(solution)/shard_map/dot_general | solution.py:54
  136.9 2.5 %fusion.4 = (f32[512]{0:T(512)S(1)}, f32[512,1152]{1,0:T(8,128)S(1)}) fusion(bf16[512,1152]{1,0:T(8,128)(2,1)S(1)} %copy-done.1, f32[512,1152]{1,0:T(8,128)S(1)} %convolution_add_fusion.1, bf16[512,1152]{1,0:T(8,128)(2,1)} %collective-permute-done.3, f32[]{:T(128)S(6)} %exp.22, f32[512,512]{1,0:T(8,128)S(1)} %copy-done.8, ...), kind=kOutput, calls=%fused_computation.21 | convolution fusion | flops 608697856 | bytes 8130564 | tf_op jit(solution)/shard_map/dot_general | solution.py:55
  139.4 1.5 fusion
  141.0 40.7 %collective-permute-done.5 = bf16[512,1152]{1,0:T(8,128)(2,1)S(1)} collective-permute-done((bf16[512,1152]{1,0:T(8,128)(2,1)S(1)}, bf16[512,1152]{1,0:T(8,128)(2,1)S(1)}, u32[]{:S(2)}, u32[]{:S(2)}) %collective-permute-start.5) | collective-permute-done | bytes 1179680 | tf_op jit(solution)/shard_map/ppermute | solution.py:9
  181.7 14.2 %collective-permute-done.4 = bf16[512,1152]{1,0:T(8,128)(2,1)S(1)} collective-permute-done((bf16[512,1152]{1,0:T(8,128)(2,1)S(1)}, bf16[512,1152]{1,0:T(8,128)(2,1)S(1)}, u32[]{:S(2)}, u32[]{:S(2)}) %collective-permute-start.4) | collective-permute-done | bytes 1179680 | tf_op jit(solution)/shard_map/ppermute | solution.py:9
  195.9 2.4 %fusion.7 = (f32[512]{0:T(512)S(1)}, f32[512,1152]{1,0:T(8,128)S(1)}) fusion(bf16[512,1152]{1,0:T(8,128)(2,1)S(1)} %copy-done, bf16[512,1152]{1,0:T(8,128)(2,1)S(1)} %collective-permute-done.5, bf16[512,1152]{1,0:T(8,128)(2,1)S(1)} %collective-permute-done.4, bf16[512,1152]{1,0:T(8,128)(2,1)S(1)} %copy-done.1, f32[512]{0:T(512)S(1)} %add_rsqrt_fusion.1, ...), kind=kOutput, calls=%fused_computation.24 | convolution fusion | flops 612236800 | bytes 8131588 | tf_op jit(solution)/shard_map/dot_general | solution.py:30
  198.3 1.8 fusion.1
  (26 shorter events, 0.7 us)
Async XLA Ops:
  0.6 1.7 copy-start
  2.3 2.7 %copy-start.2 = (s32[512]{0:T(512)S(1)}, s32[512]{0:T(512)}, u32[]{:S(2)}) copy-start(s32[512]{0:T(512)} %param.7) | copy-start | bytes 6148
  2.3 7.0 %copy-start.1 = (bf16[512,1152]{1,0:T(8,128)(2,1)S(1)}, bf16[512,1152]{1,0:T(8,128)(2,1)}, u32[]{:S(2)}) copy-start(bf16[512,1152]{1,0:T(8,128)(2,1)} %param.5) | copy-start | bytes 3538948
  2.6 51.1 %collective-permute-start.1 = (bf16[512,1152]{1,0:T(8,128)(2,1)S(1)}, bf16[512,1152]{1,0:T(8,128)(2,1)}, u32[]{:S(2)}, u32[]{:S(2)}) collective-permute-start(bf16[512,1152]{1,0:T(8,128)(2,1)S(1)} %fusion.6), channel_id=1, source_target_pairs={{0,1},{1,2},{2,3},{3,4},{4,5},{5,6},{6,7},{7,8},{8,9},{9,10},{10,1... | collective-permute-start | bytes 3538952 | tf_op jit(solution)/shard_map/ppermute | solution.py:9
  4.4 63.8 %collective-permute-start.3 = (bf16[512,1152]{1,0:T(8,128)(2,1)S(1)}, bf16[512,1152]{1,0:T(8,128)(2,1)}, u32[]{:S(2)}, u32[]{:S(2)}) collective-permute-start(bf16[512,1152]{1,0:T(8,128)(2,1)S(1)} %fusion.6), channel_id=1, source_target_pairs={{0,16},{1,17},{2,18},{3,19},{4,20},{5,21},{6,22},{7,23},{8,24},{9,... | collective-permute-start | bytes 3538952 | tf_op jit(solution)/shard_map/ppermute | solution.py:9
  5.7 62.6 %collective-permute-start.2 = (bf16[512]{0:T(512)(128)(2,1)}, bf16[512]{0:T(512)(128)(2,1)}, u32[]{:S(2)}, u32[]{:S(2)}) collective-permute-start(bf16[512]{0:T(512)(128)(2,1)} %convert_element_type.42), channel_id=1, source_target_pairs={{0,16},{1,17},{2,18},{3,19},{4,20},{5,21},{6,22},{7,23},{8,24},{9,... | collective-permute-start | bytes 3080 | tf_op jit(solution)/shard_map/ppermute | solution.py:9
  7.4 60.8 %collective-permute-start = (bf16[512]{0:T(512)(128)(2,1)}, bf16[512]{0:T(512)(128)(2,1)}, u32[]{:S(2)}, u32[]{:S(2)}) collective-permute-start(bf16[512]{0:T(512)(128)(2,1)} %convert_element_type.42), channel_id=1, source_target_pairs={{0,1},{1,2},{2,3},{3,4},{4,5},{5,6},{6,7},{7,8},{8,9},{9,10},{10,1... | collective-permute-start | bytes 3080 | tf_op jit(solution)/shard_map/ppermute | solution.py:9
  10.6 57.6 %copy-start.3 = (f32[512,512]{1,0:T(8,128)}, f32[512,512]{1,0:T(8,128)S(1)}, u32[]{:S(2)}) copy-start(f32[512,512]{1,0:T(8,128)S(1)} %fusion.10) | copy-start | bytes 3145732
  55.9 19.3 %copy-start.5 = (f32[512,512]{1,0:T(8,128)}, f32[512,512]{1,0:T(8,128)S(1)}, u32[]{:S(2)}) copy-start(f32[512,512]{1,0:T(8,128)S(1)} %fusion.9) | copy-start | bytes 3145732
  126.9 4.4 %copy-start.6 = (f32[512,512]{1,0:T(8,128)S(1)}, f32[512,512]{1,0:T(8,128)}, u32[]{:S(2)}) copy-start(f32[512,512]{1,0:T(8,128)} %copy-done.5) | copy-start | bytes 3145732
  129.4 5.2 %copy-start.7 = (f32[512,1152]{1,0:T(8,128)S(1)}, f32[512,1152]{1,0:T(8,128)}, u32[]{:S(2)}) copy-start(f32[512,1152]{1,0:T(8,128)} %fusion.18) | copy-start | bytes 7077892
  129.4 52.3 %collective-permute-start.5 = (bf16[512,1152]{1,0:T(8,128)(2,1)S(1)}, bf16[512,1152]{1,0:T(8,128)(2,1)S(1)}, u32[]{:S(2)}, u32[]{:S(2)}) collective-permute-start(bf16[512,1152]{1,0:T(8,128)(2,1)S(1)} %convolution_convert_fusion), channel_id=1, source_target_pairs={{0,16},{1,17},{2,18},{3,19},{4,20},{5,21},{6,22},{7,23},{8,24},{9,... | collective-permute-start | bytes 3538952 | tf_op jit(solution)/shard_map/ppermute | solution.py:9
  133.1 3.8 %copy-start.8 = (f32[512,512]{1,0:T(8,128)S(1)}, f32[512,512]{1,0:T(8,128)}, u32[]{:S(2)}) copy-start(f32[512,512]{1,0:T(8,128)} %get-tuple-element.23) | copy-start | bytes 3145732
  133.1 62.7 %collective-permute-start.4 = (bf16[512,1152]{1,0:T(8,128)(2,1)S(1)}, bf16[512,1152]{1,0:T(8,128)(2,1)S(1)}, u32[]{:S(2)}, u32[]{:S(2)}) collective-permute-start(bf16[512,1152]{1,0:T(8,128)(2,1)S(1)} %convolution_convert_fusion.1), channel_id=1, source_target_pairs={{0,31},{1,0},{2,1},{3,2},{4,3},{5,4},{6,5},{7,6},{8,7},{9,8},{10,9... | collective-permute-start | bytes 3538952 | tf_op jit(solution)/shard_map/ppermute | solution.py:9
  139.4 56.4 %copy-start.4 = (f32[512,512]{1,0:T(8,128)S(1)}, f32[512,512]{1,0:T(8,128)}, u32[]{:S(2)}) copy-start(f32[512,512]{1,0:T(8,128)} %copy-done.3) | copy-start | bytes 3145732
where the time goes:
time: 204 us; the launch traced here: 203 us
  waiting for transfers between devices  110 us (54%)
  blocking collectives  40.4 us (20%)
  matrix products  25.3 us (12%)
  between operations  13.1 us (6%)
  starting transfers between devices  8.15 us (4%)
  other arithmetic  6.18 us (3%)
    ppermute x6, waiting for transfers between devices, from_behind(): lax.ppermute(shard, axis, [(i, (i + by) % size) for i in range(size)])  110 us
    psum x1, blocking collectives, per_device(): lax.psum((local_totals[0], local_totals[1], local_totals[2]), 'pairs')  40.4 us
    dot_general x3, matrix products, tile(): lax.dot_general(x_block, y_block, (((1,), (1,)), ((), ())), preferred_ele...  10 us
    ppermute x6, starting transfers between devices, from_behind(): lax.ppermute(shard, axis, [(i, (i + by) % size) for i in range(size)])  8.15 us
    dot_general x3, matrix products, transposed(): lax.dot_general(weighted, x_block, (((0,), (0,)), ((), ())), preferred_el...  6.7 us
  transfers between devices with their start and end apart: 6, of which 4 were waited for; matrix products, arithmetic and copies ran while one was open for 6% of the time, Pallas kernels for 0%

commit v1 on v0

v1 whole, which is shorter than its diff:
```python
import functools

import jax
import jax.numpy as jnp
from jax import lax
from jax.experimental import pallas as pl
from jax.experimental.pallas import tpu as pltpu
from jax.sharding import PartitionSpec as P

MESH = pl.DeviceIdType.MESH
LANES = 128
F32 = jnp.float32
BF16 = jnp.bfloat16


def row_scale(rows):
    return lax.rsqrt(jnp.sum(rows * rows, axis=-1, keepdims=True) + 1e-06)


def kernel(
    n, log_scale_ref, bias_ref, lab_ref, img_hbm, txt_hbm,
    loss_ref, dscale_ref, dbias_ref, gimg_hbm, gtxt_hbm,
    img, txt, xn, yn, xscale, yscale, coltags,
    y_near, x_near, y_far, x_far, lab_prev, lab_next, lab_far,
    dx, dy, dy_near, dy_far, sums, red_out, red_in, gimg, gtxt,
    in_sem, out_sem, yf_s, yf_r, xf_s, xf_r, nr_s, nr_r, lb_s, lb_r, rd_s, rd_r,
):
    tok, width = img.shape
    chunks = tok // LANES
    me = lax.axis_index("pairs")
    after, before = lax.rem(me + 1, n), lax.rem(me + n - 1, n)
    far = lax.rem(me + n // 2, n)
    hops = [1 << s for s in range((n - 1).bit_length())]

    def flip(bit):
        return me + bit - 2 * bit * (lax.rem(me // bit, 2))

    barrier = pltpu.get_barrier_semaphore()
    greeted = [after, before, far] + [flip(b) for b in hops[1:-1]]
    for other in greeted:
        pl.semaphore_signal(barrier, inc=1, device_id=(other,), device_id_type=MESH)
    get_txt = pltpu.make_async_copy(txt_hbm, txt, in_sem.at[0])
    get_img = pltpu.make_async_copy(img_hbm, img, in_sem.at[1])
    get_txt.start()
    get_img.start()
    scale = jnp.exp(jnp.full((8, LANES), log_scale_ref[0, 0], F32))[0:1, :]
    bias = jnp.full((1, LANES), bias_ref[0, 0], F32)

    def remote(src, dst, s, r, to):
        return pltpu.make_async_remote_copy(
            src_ref=src, dst_ref=dst, send_sem=s, recv_sem=r, device_id=(to,), device_id_type=MESH
        )

    def normalized(raw, out, scales):
        @pl.loop(0, chunks)
        def _(j):
            rows = pl.ds(pl.multiple_of(j * LANES, LANES), LANES)
            value = raw[rows, :].astype(F32)
            s = row_scale(value)
            scales[rows, :] = jnp.broadcast_to(s, (LANES, LANES))
            out[rows, :] = (value * s).astype(BF16)

    def part(ref, j):
        return ref.at[pl.ds(j * LANES, LANES), :]

    y_sends = [remote(part(yn, j), part(y_far, j), yf_s.at[j], yf_r.at[j], far) for j in range(chunks)]
    x_sends = [remote(part(xn, j), part(x_far, j), xf_s.at[j], xf_r.at[j], far) for j in range(chunks)]
    y_near_send = remote(yn, y_near, nr_s.at[0], nr_r.at[0], after)
    x_near_send = remote(xn, x_near, nr_s.at[1], nr_r.at[1], before)
    lab_sends = [
        remote(lab_ref, lab_far, lb_s.at[0], lb_r.at[0], far),
        remote(lab_ref, lab_prev, lb_s.at[1], lb_r.at[1], after),
        remote(lab_ref, lab_next, lb_s.at[2], lb_r.at[2], before),
    ]

    get_txt.wait()
    normalized(txt, yn, yscale)
    pl.semaphore_wait(barrier, len(greeted))
    for c in lab_sends:
        c.start()
    for c in y_sends:
        c.start()
    y_near_send.start()
    get_img.wait()
    normalized(img, xn, xscale)
    x_near_send.start()

    for j in range(chunks):
        row = jnp.broadcast_to(lab_ref[j : j + 1, :].astype(F32), (LANES, LANES))
        coltags[j * LANES : (j + 1) * LANES, :] = row.T
    for ref in (dx, dy, dy_near, dy_far, sums):
        ref[...] = jnp.zeros_like(ref)

    def side(local, incoming, labels, total, j, count, with_sums):
        cols = pl.ds(pl.multiple_of(j * count * LANES, count * LANES), count * LANES)

        @pl.loop(0, 2)
        def _(b):
            rows = pl.ds(pl.multiple_of(b * (tok // 2), tok // 2), tok // 2)
            block = incoming[cols, :]
            cosine = lax.dot_general(
                local[rows, :], block, (((1,), (1,)), ((), ())), preferred_element_type=F32
            )
            weights = []
            for c in range(count):
                tags = labels[pl.ds(j * count + c, 1), :].astype(F32)
                logits = scale * cosine[:, c * LANES : (c + 1) * LANES] + bias
                same = coltags[rows, :] == tags
                margin = jnp.where(same, logits, -logits)
                e = jnp.exp(-jnp.abs(logits))
                r = 1.0 / (1.0 + e)
                sig = jnp.where(margin >= 0.0, e * r, r)
                slope = jnp.where(same, -sig, sig)
                weights.append((scale * slope).astype(BF16))
                if with_sums:
                    term = jnp.maximum(-margin, 0.0) + jnp.log1p(e)
                    for i, v in enumerate((term, slope * (logits - bias), slope)):
                        sums[i] += jnp.sum(v.reshape(-1, 8, LANES), axis=0)
            weighted = weights[0] if count == 1 else jnp.concatenate(weights, axis=1)
            total[rows, :] += jnp.dot(weighted, block, preferred_element_type=F32)

    def whole(local, incoming, labels, total, with_sums):
        @pl.loop(0, chunks // 2)
        def _(j):
            side(local, incoming, labels, total, j, 2, with_sums)

    def pulled(raw, scales, grad_of, out, hbm, first_sem):
        copies = []
        for j in range(chunks):
            rows = pl.ds(j * LANES, LANES)
            g = grad_of(rows)
            value = raw[rows, :].astype(F32)
            s = scales[rows, 0:1]
            dots = jnp.sum(g * value, axis=-1, keepdims=True)
            out[rows, :] = (s * g - value * (s * s * s * dots)).astype(BF16)
            copy = pltpu.make_async_copy(out.at[rows, :], hbm.at[rows, :], out_sem.at[first_sem + j])
            copy.start()
            copies.append(copy)
        return copies

    whole(xn, yn, lab_ref, dx, True)
    whole(yn, xn, lab_ref, dy, False)
    for j in range(chunks):
        y_sends[j].wait_send()
        x_sends[j].start()
        y_sends[j].wait_recv()
        if j == 0:
            lab_sends[0].wait_recv()
        side(xn, y_far, lab_far, dx, j, 1, True)
    lab_sends[1].wait_recv()
    y_near_send.wait_recv()
    whole(xn, y_near, lab_prev, dx, True)

    row = lax.broadcasted_iota(jnp.int32, (8, LANES), 0)
    s0, s1, s2 = (jnp.sum(sums[i]) for i in range(3))
    mine = jnp.where(row == 0, s0, jnp.where(row == 1, s1, s2))
    lab_sends[2].wait_recv()
    x_near_send.wait_recv()
    for step, bit in enumerate(hops):
        red_out[step] = mine
        copy = remote(red_out.at[step], red_in.at[step], rd_s.at[step], rd_r.at[step], flip(bit))
        copy.start()
        if step == 0:
            whole(yn, x_near, lab_next, dy_near, False)
        if step == 1:
            out_copies = pulled(img, xscale, lambda rows: dx[rows, :], gimg, gimg_hbm, 0)
        if step == 2:
            dy[...] += dy_near[...].astype(BF16).astype(F32)
        copy.wait()
        mine = mine + red_in[step]
    inverse = 1.0 / (n * tok)
    loss_ref[0, 0] = mine[0, 0] * inverse
    dscale_ref[0, 0] = mine[1, 0] * inverse
    dbias_ref[0, 0] = mine[2, 0] * inverse

    for j in range(chunks):
        x_sends[j].wait_recv()
        side(yn, x_far, lab_far, dy_far, j, 1, False)

    def text_dy(rows):
        return dy[rows, :] + dy_far[rows, :].astype(BF16).astype(F32)

    out_copies += pulled(txt, yscale, text_dy, gtxt, gtxt_hbm, chunks)
    for c in x_sends + lab_sends + [y_near_send, x_near_send]:
        c.wait_send()
    for c in out_copies:
        c.wait()


def per_device(n, images, texts, labels, log_scale, bias):
    tok, width = images.shape
    chunks = tok // LANES
    steps = (n - 1).bit_length()
    smem = pl.BlockSpec(memory_space=pltpu.SMEM)
    vmem = pl.BlockSpec(memory_space=pltpu.VMEM)
    hbm = pl.BlockSpec(memory_space=pltpu.HBM)
    half = lambda: pltpu.VMEM((tok, width), BF16)
    full = lambda: pltpu.VMEM((tok, width), F32)
    tags = lambda: pltpu.VMEM((chunks, LANES), jnp.int32)
    wide = lambda: pltpu.VMEM((tok, LANES), F32)
    dma = lambda k: pltpu.SemaphoreType.DMA((k,))
    scalar = jax.ShapeDtypeStruct((1, 1), F32)
    block = jax.ShapeDtypeStruct((tok, width), BF16)
    loss, dscale, dbias, gimg, gtxt = pl.pallas_call(
        functools.partial(kernel, n),
        out_shape=(scalar, scalar, scalar, block, block),
        in_specs=[smem, smem, vmem, hbm, hbm],
        out_specs=(smem, smem, smem, hbm, hbm),
        scratch_shapes=[
            half(), half(), half(), half(), wide(), wide(), wide(),
            half(), half(), half(), half(), tags(), tags(), tags(),
            full(), full(), full(), full(), pltpu.VMEM((3, 8, LANES), F32),
            pltpu.VMEM((steps, 8, LANES), F32), pltpu.VMEM((steps, 8, LANES), F32), half(), half(),
            dma(2), dma(2 * chunks), dma(chunks), dma(chunks), dma(chunks), dma(chunks),
            dma(2), dma(2), dma(3), dma(3), dma(steps), dma(steps),
        ],
        compiler_params=pltpu.CompilerParams(
            collective_id=0, has_side_effects=True, vmem_limit_bytes=48 * 1024 * 1024
        ),
    )(log_scale.reshape(1, 1), bias.reshape(1, 1), labels.reshape(chunks, LANES), images, texts)
    return (loss.reshape(()), dscale.reshape(()), dbias.reshape(()), gimg, gtxt)


def solution(mesh):
    placed = (P("pairs", None), P("pairs", None), P("pairs"), P(), P())
    return jax.shard_map(
        functools.partial(per_device, mesh.shape["pairs"]),
        mesh=mesh,
        in_specs=placed,
        out_specs=(P(), P(), P(), P("pairs", None), P("pairs", None)),
        check_vma=False,
    )
```

time: 204 us -> 147 us (0.72)
  the two profiles are of different devices: /device:TPU:15 before, /device:TPU:0 now
where the time goes in v1:
time: 147 us; the launch traced here: 146 us
  Pallas kernels  133 us (90%)
  between operations  7.11 us (5%)
  local copies, waits for them, and re-layouts  5.24 us (4%)
    pallas_call x1, Pallas kernels, per_device(): pl.pallas_call(functools.partial(kernel, n), out_shape=(scalar, scalar, s...  133 us
    unnamed x8, local copies, waits for them, and re-layouts  5.24 us

profile of v1, /device:TPU:0, one launch (start us, length us, event | category | flops | bytes accessed | tf_op | source)
XLA Modules:
  0.0 145.8 jit_solution(10063533026435951586)
XLA Ops:
  1.9 0.0 copy-start
  1.9 1.3 copy-done
  3.2 0.0 copy-start.1
  3.2 1.3 copy-done.1
  4.5 0.0 copy-start.2
  4.5 0.7 copy-done.2
  5.1 133.4 %shard_map.92 = (f32[1,1]{1,0:T(1,128)}, f32[1,1]{1,0:T(1,128)}, f32[1,1]{1,0:T(1,128)}, bf16[512,1152]{1,0:T(8,128)(2,1)S(1)}, bf16[512,1152]{1,0:T(8,128)(2,1)S(1)}) custom-call(f32[1,1]{1,0:T(1,128)} %bitcast.6.log_scale_ref, f32[1,1]{1,0:T(1,128)} %bitcast.7.bias_ref, s32[4,128]{1,0:T(4,128)S(1)} %bitcast.8, bf16[512,1152]{1,0:T(8,128)(2,1)S(1)} %copy-done, ...), custom_call_target="tpu_custom_call" | custom-call | tf_op jit(solution)/shard_map/pallas_call | solution.py:204
  140.3 1.0 copy.20
  141.3 1.0 copy.21
Async XLA Ops:
  1.9 1.3 copy-start
  3.2 1.3 copy-start.1
  4.5 0.7 copy-start.2

commit v2 on v1

--- a/solution.py
+++ b/solution.py
@@ -21,9 +21,9 @@
     n, log_scale_ref, bias_ref, lab_ref, img_hbm, txt_hbm,
     loss_ref, dscale_ref, dbias_ref, gimg_hbm, gtxt_hbm,
     img, txt, xn, yn, xscale, yscale, coltags,
-    y_near, x_near, y_far, x_far, lab_prev, lab_next, lab_far,
+    y_near, x_near, y_far, x_far, relay, lab_prev, lab_next, lab_far,
     dx, dy, dy_near, dy_far, sums, red_out, red_in, gimg, gtxt,
-    in_sem, out_sem, yf_s, yf_r, xf_s, xf_r, nr_s, nr_r, lb_s, lb_r, rd_s, rd_r,
+    in_sem, out_sem, yf_s, yf_r, xf_s, xf_r, nr_s, nr_r, lb_s, lb_r, rd_s, rd_r, rl_s, rl_r,
 ):
     tok, width = img.shape
     chunks = tok // LANES
@@ -35,8 +35,15 @@
     def flip(bit):
         return me + bit - 2 * bit * (lax.rem(me // bit, 2))
 
+    relayed = n == 32
+    place = lax.rem(me, n // 2)
+    across = lax.rem(jnp.where(place < n // 4, me + n - 3, me + 3), n)
+    first, last = place == 0, place == n // 2 - 1
+    relays_x, relays_y = place == 2, place == n // 2 - 3
     barrier = pltpu.get_barrier_semaphore()
     greeted = [after, before, far] + [flip(b) for b in hops[1:-1]]
+    if relayed:
+        greeted += [lax.rem(me + 3, n), lax.rem(me + n - 3, n)]
     for other in greeted:
         pl.semaphore_signal(barrier, inc=1, device_id=(other,), device_id_type=MESH)
     get_txt = pltpu.make_async_copy(txt_hbm, txt, in_sem.at[0])
@@ -65,8 +72,29 @@
 
     y_sends = [remote(part(yn, j), part(y_far, j), yf_s.at[j], yf_r.at[j], far) for j in range(chunks)]
     x_sends = [remote(part(xn, j), part(x_far, j), xf_s.at[j], xf_r.at[j], far) for j in range(chunks)]
-    y_near_send = remote(yn, y_near, nr_s.at[0], nr_r.at[0], after)
-    x_near_send = remote(xn, x_near, nr_s.at[1], nr_r.at[1], before)
+    def half(ref, h):
+        return ref.at[pl.ds(h * (tok // 2), tok // 2), :]
+
+    y_near_sends = [remote(half(yn, h), half(y_near, h), nr_s.at[h], nr_r.at[h], after) for h in range(2)]
+    x_near_sends = [remote(half(xn, h), half(x_near, h), nr_s.at[2 + h], nr_r.at[2 + h], before) for h in range(2)]
+    y_detour = remote(half(yn, 1), relay, nr_s.at[1], rl_r.at[0], flip(2))
+    x_detour = remote(half(xn, 1), relay, nr_s.at[3], rl_r.at[0], flip(2))
+    y_forward = remote(relay, half(y_near, 1), rl_s.at[0], nr_r.at[1], across)
+    x_forward = remote(relay, half(x_near, 1), rl_s.at[0], nr_r.at[3], across)
+
+    def send_near(sends, detour, detoured):
+        sends[0].start()
+        if relayed:
+            @pl.when(detoured)
+            def _():
+                detour.start()
+
+            @pl.when(jnp.logical_not(detoured))
+            def _():
+                sends[1].start()
+        else:
+            sends[1].start()
+
     lab_sends = [
         remote(lab_ref, lab_far, lb_s.at[0], lb_r.at[0], far),
         remote(lab_ref, lab_prev, lb_s.at[1], lb_r.at[1], after),
@@ -78,12 +106,12 @@
     pl.semaphore_wait(barrier, len(greeted))
     for c in lab_sends:
         c.start()
+    send_near(y_near_sends, y_detour, last)
     for c in y_sends:
         c.start()
-    y_near_send.start()
     get_img.wait()
     normalized(img, xn, xscale)
-    x_near_send.start()
+    send_near(x_near_sends, x_detour, first)
 
     for j in range(chunks):
         row = jnp.broadcast_to(lab_ref[j : j + 1, :].astype(F32), (LANES, LANES))
@@ -139,23 +167,37 @@
         return copies
 
     whole(xn, yn, lab_ref, dx, True)
+    if relayed:
+        @pl.when(relays_y)
+        def _():
+            y_detour.wait_recv()
+            y_forward.start()
+
+        @pl.when(relays_x)
+        def _():
+            x_detour.wait_recv()
+            x_forward.start()
+
     whole(yn, xn, lab_ref, dy, False)
     for j in range(chunks):
         y_sends[j].wait_send()
-        x_sends[j].start()
+        if j > 0:
+            x_sends[j - 1].start()
         y_sends[j].wait_recv()
         if j == 0:
             lab_sends[0].wait_recv()
         side(xn, y_far, lab_far, dx, j, 1, True)
     lab_sends[1].wait_recv()
-    y_near_send.wait_recv()
+    for c in y_near_sends:
+        c.wait_recv()
     whole(xn, y_near, lab_prev, dx, True)
 
     row = lax.broadcasted_iota(jnp.int32, (8, LANES), 0)
     s0, s1, s2 = (jnp.sum(sums[i]) for i in range(3))
     mine = jnp.where(row == 0, s0, jnp.where(row == 1, s1, s2))
     lab_sends[2].wait_recv()
-    x_near_send.wait_recv()
+    for c in x_near_sends:
+        c.wait_recv()
     for step, bit in enumerate(hops):
         red_out[step] = mine
         copy = remote(red_out.at[step], red_in.at[step], rd_s.at[step], rd_r.at[step], flip(bit))
@@ -173,6 +215,8 @@
     dscale_ref[0, 0] = mine[1, 0] * inverse
     dbias_ref[0, 0] = mine[2, 0] * inverse
 
+    x_sends[0].wait_send()
+    x_sends[chunks - 1].start()
     for j in range(chunks):
         x_sends[j].wait_recv()
         side(yn, x_far, lab_far, dy_far, j, 1, False)
@@ -181,8 +225,13 @@
         return dy[rows, :] + dy_far[rows, :].astype(BF16).astype(F32)
 
     out_copies += pulled(txt, yscale, text_dy, gtxt, gtxt_hbm, chunks)
-    for c in x_sends + lab_sends + [y_near_send, x_near_send]:
+    for c in x_sends[1:] + lab_sends + y_near_sends + x_near_sends:
         c.wait_send()
+    if relayed:
+        @pl.when(relays_y | relays_x)
+        def _():
+            y_forward.wait_send()
+
     for c in out_copies:
         c.wait()
 
@@ -208,14 +257,14 @@
         out_specs=(smem, smem, smem, hbm, hbm),
         scratch_shapes=[
             half(), half(), half(), half(), wide(), wide(), wide(),
-            half(), half(), half(), half(), tags(), tags(), tags(),
+            half(), half(), half(), half(), pltpu.VMEM((tok // 2, width), BF16), tags(), tags(), tags(),
             full(), full(), full(), full(), pltpu.VMEM((3, 8, LANES), F32),
             pltpu.VMEM((steps, 8, LANES), F32), pltpu.VMEM((steps, 8, LANES), F32), half(), half(),
             dma(2), dma(2 * chunks), dma(chunks), dma(chunks), dma(chunks), dma(chunks),
-            dma(2), dma(2), dma(3), dma(3), dma(steps), dma(steps),
+            dma(4), dma(4), dma(3), dma(3), dma(steps), dma(steps), dma(1), dma(1),
         ],
         compiler_params=pltpu.CompilerParams(
-            collective_id=0, has_side_effects=True, vmem_limit_bytes=48 * 1024 * 1024
+            collective_id=0, has_side_effects=True, vmem_limit_bytes=60 * 1024 * 1024
         ),
     )(log_scale.reshape(1, 1), bias.reshape(1, 1), labels.reshape(chunks, LANES), images, texts)
     return (loss.reshape(()), dscale.reshape(()), dbias.reshape(()), gimg, gtxt)

time: 147 us -> 136 us (0.925)
  Pallas kernels: 133 us -> 125 us
  local copies, waits for them, and re-layouts: 5.24 us -> 3.49 us
    pallas_call x1, Pallas kernels: 133 us -> 125 us  [per_device(): pl.pallas_call(functools.partial(kernel, n), out_shape=(scalar, scalar, s...]
    unnamed x8 -> x4, local copies, waits for them, and re-layouts: 5.24 us -> 3.49 us
where the time goes in v2:
time: 136 us
  Pallas kernels  125 us (92%)
  between operations  7.24 us (5%)
  local copies, waits for them, and re-layouts  3.49 us (3%)
    pallas_call x1, Pallas kernels, per_device(): pl.pallas_call(functools.partial(kernel, n), out_shape=(scalar, scalar, s...  125 us
    unnamed x4, local copies, waits for them, and re-layouts  3.49 us

profile of v2, /device:TPU:0, one launch (start us, length us, event | category | flops | bytes accessed | tf_op | source)
XLA Modules:
  0.0 135.6 jit_solution(8830095147995667103)
XLA Ops:
  1.9 124.8 %shard_map.92 = (f32[1,1]{1,0:T(1,128)}, f32[1,1]{1,0:T(1,128)}, f32[1,1]{1,0:T(1,128)}, bf16[512,1152]{1,0:T(8,128)(2,1)}, bf16[512,1152]{1,0:T(8,128)(2,1)}) custom-call(f32[1,1]{1,0:T(1,128)} %bitcast.6.log_scale_ref, f32[1,1]{1,0:T(1,128)} %bitcast.7.bias_ref, s32[4,128]{1,0:T(4,128)} %bitcast.8, bf16[512,1152]{1,0:T(8,128)(2,1)} %img_hbm.1, ...), custom_call_target="tpu_custom_call" | custom-call | tf_op jit(solution)/shard_map/pallas_call | solution.py:253
  128.7 0.0 copy-start
  128.7 2.5 %copy.20 = bf16[512,1152]{1,0:T(8,128)(2,1)} copy(bf16[512,1152]{1,0:T(8,128)(2,1)} %get-tuple-element.23) | data formatting | bytes 2359296
  131.2 0.0 copy-done
  131.2 1.0 copy.21
Async XLA Ops:
  128.7 2.5 %copy-start = (bf16[512,1152]{1,0:T(8,128)(2,1)S(1)}, bf16[512,1152]{1,0:T(8,128)(2,1)}, u32[]{:S(2)}) copy-start(bf16[512,1152]{1,0:T(8,128)(2,1)} %get-tuple-element.24) | copy-start | bytes 3538948

commit v3 on v2

--- a/solution.py
+++ b/solution.py
@@ -107,11 +107,11 @@
     for c in lab_sends:
         c.start()
     send_near(y_near_sends, y_detour, last)
-    for c in y_sends:
-        c.start()
     get_img.wait()
     normalized(img, xn, xscale)
     send_near(x_near_sends, x_detour, first)
+    for c in y_sends:
+        c.start()
 
     for j in range(chunks):
         row = jnp.broadcast_to(lab_ref[j : j + 1, :].astype(F32), (LANES, LANES))
@@ -198,6 +198,8 @@
     lab_sends[2].wait_recv()
     for c in x_near_sends:
         c.wait_recv()
+    layer = me // (n // 4)
+    inner = (layer == 1) | (layer == 2)
     for step, bit in enumerate(hops):
         red_out[step] = mine
         copy = remote(red_out.at[step], red_in.at[step], rd_s.at[step], rd_r.at[step], flip(bit))
@@ -206,6 +208,12 @@
             whole(yn, x_near, lab_next, dy_near, False)
         if step == 1:
             out_copies = pulled(img, xscale, lambda rows: dx[rows, :], gimg, gimg_hbm, 0)
+        if step == 3:
+            @pl.when(inner)
+            def _():
+                x_sends[0].wait_send()
+                x_sends[chunks - 1].start()
+
         if step == 2:
             dy[...] += dy_near[...].astype(BF16).astype(F32)
         copy.wait()
@@ -215,8 +223,11 @@
     dscale_ref[0, 0] = mine[1, 0] * inverse
     dbias_ref[0, 0] = mine[2, 0] * inverse
 
-    x_sends[0].wait_send()
-    x_sends[chunks - 1].start()
+    @pl.when(jnp.logical_not(inner))
+    def _():
+        x_sends[0].wait_send()
+        x_sends[chunks - 1].start()
+
     for j in range(chunks):
         x_sends[j].wait_recv()
         side(yn, x_far, lab_far, dy_far, j, 1, False)

time: 136 us -> 131 us (0.963)
  Pallas kernels: 125 us -> 119 us
    pallas_call x1, Pallas kernels: 125 us -> 119 us  [per_device(): pl.pallas_call(functools.partial(kernel, n), out_shape=(scalar, scalar, s...]
where the time goes in v3:
time: 131 us; the launch traced here: 130 us
  Pallas kernels  119 us (91%)
  between operations  7.24 us (6%)
  local copies, waits for them, and re-layouts  3.49 us (3%)
    pallas_call x1, Pallas kernels, per_device(): pl.pallas_call(functools.partial(kernel, n), out_shape=(scalar, scalar, s...  119 us
    unnamed x4, local copies, waits for them, and re-layouts  3.49 us

profile of v3, /device:TPU:0, one launch (start us, length us, event | category | flops | bytes accessed | tf_op | source)
XLA Modules:
  0.0 129.7 jit_solution(5398945271492513542)
XLA Ops:
  1.9 119.0 %shard_map.92 = (f32[1,1]{1,0:T(1,128)}, f32[1,1]{1,0:T(1,128)}, f32[1,1]{1,0:T(1,128)}, bf16[512,1152]{1,0:T(8,128)(2,1)}, bf16[512,1152]{1,0:T(8,128)(2,1)}) custom-call(f32[1,1]{1,0:T(1,128)} %bitcast.6.log_scale_ref, f32[1,1]{1,0:T(1,128)} %bitcast.7.bias_ref, s32[4,128]{1,0:T(4,128)} %bitcast.8, bf16[512,1152]{1,0:T(8,128)(2,1)} %img_hbm.1, ...), custom_call_target="tpu_custom_call" | custom-call | tf_op jit(solution)/shard_map/pallas_call | solution.py:264
  122.9 0.0 copy-start
  122.9 2.5 %copy.20 = bf16[512,1152]{1,0:T(8,128)(2,1)} copy(bf16[512,1152]{1,0:T(8,128)(2,1)} %get-tuple-element.23) | data formatting | bytes 2359296
  125.3 0.0 copy-done
  125.3 1.0 copy.21
Async XLA Ops:
  122.9 2.5 %copy-start = (bf16[512,1152]{1,0:T(8,128)(2,1)S(1)}, bf16[512,1152]{1,0:T(8,128)(2,1)}, u32[]{:S(2)}) copy-start(bf16[512,1152]{1,0:T(8,128)(2,1)} %get-tuple-element.24) | copy-start | bytes 3538948
